TPU v7x, 32 devices: a whole 2x2x4 slice. The times are simulated.
32 devices in a mesh: seq: 8 (over y, x, core), chan: 4 (over z).
Axes of the slice: x: 2, y: 2, z: 4, core: 2. Of those that a mesh axis runs over, the one named last changes fastest.
Arguments:
- token_ids: int32 [4096], P('seq'), may hold values from 0 to 511
- embed_table: bfloat16 [512, 4096], replicated, may hold values from -6 to 6
- in_weight: bfloat16 [4096, 3, 2048], P(None, None, 'chan'), may hold values from -0.09375 to 0.09375
- short_filter: float32 [3, 3, 2048], P(None, None, 'chan'), may hold values from -3 to 3
- long_filter: float32 [4096, 2048], P('seq', 'chan'), may hold values from -1.5 to 1.5
- skip_gain: float32 [2048], P('chan'), may hold values from -4 to 4
- out_weight: bfloat16 [2048, 4096], P('chan'), may hold values from -0.125 to 0.125
Outputs:
- mixed: bfloat16 [4096, 4096], P(('seq', 'chan'))
All inputs are finite; a program needn't handle non-finite values.
Results may differ from a plain program's by a relative error of at most 0.0072.
Values may be sent and summed in bfloat16 or wider, within the bound.
A program may use at most 128 MiB of HBM per device.

v0:
```python
import functools

import jax
import jax.numpy as jnp
import numpy as np
from jax import lax
from jax.experimental import pallas as pl
from jax.experimental.pallas import tpu as pltpu
from jax.sharding import PartitionSpec as P

HIGHEST = lax.Precision.HIGHEST
LANES = 128
INNER = 64


def transform_matrices(length):
    outer = length // INNER
    n1 = np.arange(outer)[None, :]
    k1 = np.arange(outer)[:, None] + 0.5
    angle = 2.0 * np.pi * n1 * k1 / (2 * outer)
    first = np.concatenate([np.cos(angle), -np.sin(angle)], 0)
    n2 = np.arange(INNER)[None, None, :]
    k2 = np.arange(INNER)[None, :, None]
    turn = 2.0 * np.pi * n2 * (k1[:, :, None] + 2 * outer * k2) / (2 * length)
    cosine, sine = np.cos(turn), -np.sin(turn)
    second = np.concatenate(
        [np.concatenate([cosine, -sine], 2), np.concatenate([sine, cosine], 2)], 1
    )
    last = first.T / length
    return (
        first.astype(np.float32),
        second.astype(np.float32),
        np.swapaxes(second, 1, 2).astype(np.float32),
        last.astype(np.float32),
    )


def dot32(left, right):
    return jnp.dot(left, right, precision=HIGHEST, preferred_element_type=jnp.float32)


def operator_kernel(
    width, ids_ref, table_ref, taps_ref, skip_ref, filter_ref, first_ref, second_ref, back_ref, last_ref,
    out_ref, projected, signal, gate, work
):
    length = ids_ref.shape[0]
    vocab = table_ref.shape[0]
    outer = length // INNER
    chunk = min(512, length)
    tap_count = taps_ref.shape[0] // 3
    projected[pl.ds(0, 8), :] = jnp.zeros((8, projected.shape[1]), jnp.float32)

    @pl.loop(0, length // chunk)
    def _(step):
        start = pl.multiple_of(step * chunk, chunk)
        rows = pl.ds(start, chunk)
        chosen = lax.broadcasted_iota(jnp.int32, (chunk, vocab), 1) == ids_ref[rows, :]
        projected[pl.ds(start + 8, chunk), :] = jnp.dot(
            chosen.astype(jnp.float32).astype(jnp.bfloat16), table_ref[...], preferred_element_type=jnp.float32
        )
        window = projected[pl.ds(start, chunk + 8), :]
        branches = []
        for branch in range(3):
            total = jnp.zeros((chunk, LANES), jnp.float32)
            for tap in range(tap_count):
                part = window[8 - tap : 8 - tap + chunk, branch * LANES : (branch + 1) * LANES]
                row = tap * 3 + branch
                total = total + taps_ref[row : row + 1, :] * part
            branches.append(total)
        gate[rows, :] = branches[1]
        signal[rows, :] = branches[0] * branches[2] + filter_ref[rows, :].astype(jnp.float32)

    @pl.loop(0, INNER, unroll=4)
    def _(n2):
        work[pl.ds(n2 * (2 * outer), 2 * outer), :] = dot32(
            first_ref[...], signal[pl.ds(n2, outer, stride=INNER), :]
        )

    @pl.loop(0, outer, unroll=4)
    def _(k1):
        real_rows = pl.ds(k1, INNER, stride=2 * outer)
        imag_rows = pl.ds(k1 + outer, INNER, stride=2 * outer)
        spectrum = dot32(
            second_ref[k1], jnp.concatenate([work[real_rows, :], work[imag_rows, :]], 0)
        )
        turned = pltpu.roll(spectrum, LANES - width, 1)
        real, imag = spectrum[:INNER], spectrum[INNER:]
        other_real, other_imag = turned[:INNER], turned[INNER:]
        product = jnp.concatenate(
            [real * other_real - imag * other_imag, real * other_imag + imag * other_real], 0
        )
        result = dot32(back_ref[k1], product)
        work[real_rows, :] = result[:INNER]
        work[imag_rows, :] = result[INNER:]

    @pl.loop(0, INNER, unroll=4)
    def _(n2):
        rows = pl.ds(n2, outer, stride=INNER)
        convolved = dot32(last_ref[...], work[pl.ds(n2 * (2 * outer), 2 * outer), :])
        signal[rows, :] = gate[rows, :] * (convolved + skip_ref[0:1, :] * signal[rows, :])

    out_ref[...] = signal[...].astype(jnp.bfloat16)


def run_operator(ids, table, taps, skip, filters, width):
    length = ids.shape[0]
    outer = length // INNER
    matrices = transform_matrices(length)
    spec = pl.BlockSpec(memory_space=pltpu.VMEM)
    return pl.pallas_call(
        functools.partial(operator_kernel, width),
        out_shape=jax.ShapeDtypeStruct((length, LANES), jnp.bfloat16),
        in_specs=[spec] * 9,
        out_specs=spec,
        scratch_shapes=[
            pltpu.VMEM((length + 8, 3 * LANES), jnp.float32),
            pltpu.VMEM((length, LANES), jnp.float32),
            pltpu.VMEM((length, LANES), jnp.float32),
            pltpu.VMEM((2 * length, LANES), jnp.float32),
        ],
        compiler_params=pltpu.CompilerParams(vmem_limit_bytes=60 * 2**20),
        cost_estimate=pl.CostEstimate(flops=10**10, bytes_accessed=2 * 10**7, transcendentals=0),
    )(ids, table, taps, skip, filters, *[jnp.asarray(m) for m in matrices])


def to_lanes(array, before=0):
    pads = [(0, 0)] * (array.ndim - 1) + [(before, LANES - before - array.shape[-1])]
    return jnp.pad(array, pads)


def body(token_ids, embed_table, in_weight, short_filter, long_filter, skip_gain, out_weight):
    place = lax.axis_index("seq")
    seq_count, chan_count = lax.axis_size("seq"), lax.axis_size("chan")
    depth = embed_table.shape[1]
    width = in_weight.shape[2] // seq_count
    columns = out_weight.shape[1] // seq_count

    out_part = lax.dynamic_slice_in_dim(out_weight, place * columns, columns, 1)
    out_all = lax.all_gather(out_part, "chan", axis=0, tiled=False)

    filters = lax.all_to_all(long_filter.astype(jnp.bfloat16), "seq", split_axis=1, concat_axis=0, tiled=True)
    ids = lax.all_gather(token_ids, "seq", axis=0, tiled=True)
    length = ids.shape[0]

    def mine(array):
        return lax.dynamic_slice_in_dim(array, place * width, width, array.ndim - 1)

    table = jnp.einsum(
        "vd,dgc->vgc", embed_table, mine(in_weight), preferred_element_type=jnp.float32
    ).astype(jnp.bfloat16)
    table = to_lanes(table).reshape(embed_table.shape[0], -1)
    taps = to_lanes(mine(short_filter)).reshape(-1, LANES)
    skip = to_lanes(mine(skip_gain)[None])
    carried = run_operator(ids[:, None], table, taps, skip, to_lanes(filters, width), width)[:, :width]

    rows = length // (seq_count * chan_count)
    blocks = carried.reshape(seq_count, chan_count, rows, width)
    blocks = lax.all_to_all(blocks, "chan", split_axis=1, concat_axis=1, tiled=True)
    blocks = blocks.transpose(0, 2, 1, 3).reshape(seq_count * rows, chan_count * width)
    carried_all = lax.all_gather(blocks, "seq", axis=0, tiled=False)
    weight = out_all.reshape(chan_count, seq_count, width, columns).transpose(1, 0, 2, 3)
    weight = weight.reshape(seq_count, chan_count * width, columns)
    mixed = jnp.einsum("stk,skn->tn", carried_all, weight, preferred_element_type=jnp.float32)
    mixed = mixed.astype(jnp.bfloat16).reshape(seq_count, rows, columns)
    mixed = lax.all_to_all(mixed, "seq", split_axis=0, concat_axis=2, tiled=True)
    return mixed[0]


def solution(mesh):
    return jax.shard_map(
        body,
        mesh=mesh,
        in_specs=(
            P("seq"),
            P(),
            P(None, None, "chan"),
            P(None, None, "chan"),
            P("seq", "chan"),
            P("chan"),
            P("chan", None),
        ),
        out_specs=P(("seq", "chan"), None),
        check_vma=False,
    )
```

profile of v0, /device:TPU:0, one launch (start us, length us, event | category | flops | bytes accessed | tf_op | source)
XLA Modules:
  0.0 169.5 jit_solution(520279902433328205)
XLA Ops:
  6.5 0.0 copy-start
  6.5 0.0 all-gather.7.cloned.1.call-start
  6.5 1.9 %constant_dynamic-slice_fusion = bf16[512,512]{1,0:T(8,128)(2,1)} fusion(bf16[512,4096]{1,0:T(8,128)(2,1)} %param.17, s32[]{:T(128)S(6)} %select_n.9), kind=kLoop, calls=%fused_computation.6 | loop fusion | bytes 1048580 | tf_op jit(solution)/shard_map/dynamic_slice | solution.py:138
  8.4 0.0 all-gather.7.cloned.1.call-update
  8.5 2.2 %copy.28 = bf16[512,512]{0,1:T(8,128)(2,1)} copy(f32[512,512]{1,0:T(8,128)} %param.15) | data formatting | bytes 1572864 | tf_op args[4]
  10.7 5.2 %all-to-all-start = ((bf16[512,8,64]{0,2,1:T(8,128)(2,1)}), bf16[512,8,64]{0,2,1:T(8,128)(2,1)S(1)}, u32[]{:S(2)}, u32[]{:S(2)}) async-start(bf16[512,8,64]{0,2,1:T(8,128)(2,1)} %bitcast.6), calls=%async_computation | async-start | bytes 1048576 | tf_op jit(solution)/shard_map/all_to_all | solution.py:141
  15.9 0.0 all-gather.5.cloned.1.call-start
  15.9 0.0 copy-done
  15.9 0.1 constant_dynamic-slice_fusion.1
  16.0 0.8 dynamic-slice_bitcast_fusion
  16.8 0.5 pad.18.skip_ref
  17.3 0.6 reshape.23.taps_ref
  17.9 0.0 copy-start.1
  17.9 6.3 %fusion.8 = bf16[512,3,64]{0,2,1:T(8,128)(2,1)S(1)} fusion(bf16[512,4096]{1,0:T(8,128)(2,1)} %param.12, bf16[4096,3,512]{2,0,1:T(8,128)(2,1)} %param.13, s32[]{:T(128)S(6)} %select_n.8), kind=kOutput, calls=%fused_computation.5 | convolution fusion | flops 805404672 | bytes 7536644 | tf_op jit(solution)/shard_map/vd,dgc->vgc/dot_general | solution.py:148
  24.3 0.9 copy.31.table_ref
  25.2 0.0 copy-done.1
  25.2 9.3 %all-gather.1 = s32[8,1,512]{2,1,0:T(1,128)S(1)} all-gather(s32[1,1,512]{2,1,0:T(1,128)S(1)} %bitcast.51), channel_id=1, replica_groups=mesh['seq'=8,'chan'=4] {'seq'}, dimensions={0}, use_global_device_ids=true | all-gather | bytes 18432 | tf_op jit(solution)/shard_map/all_gather | solution.py:142
  34.5 2.0 %copy.30.ids_ref = s32[4096,1]{1,0:T(8,128)} copy(s32[4096,1]{0,1:T(1,128)S(1)} %bitcast.50) | data formatting | bytes 32768 | tf_op jit(solution)/shard_map/broadcast_in_dim | solution.py:154
  36.5 0.0 all-to-all-done
  36.5 0.5 copy.29
  37.0 1.4 pad.19.filter_ref
  38.4 43.4 %shard_map.109 = bf16[4096,128]{1,0:T(8,128)(2,1)} custom-call(s32[4096,1]{1,0:T(8,128)} %copy.30.ids_ref, bf16[512,384]{1,0:T(8,128)(2,1)} %copy.31.table_ref, f32[9,128]{1,0:T(8,128)} %reshape.23.taps_ref, f32[1,128]{1,0:T(1,128)} %pad.18.skip_ref, bf16[4096,128]{1,0:T(8,128)(2,1)} %pad.19.filter_ref, f32[128,64]{1,0:T(8,128)} %constant.26.clone.first_ref, ...), custom_call_target="tpu_custom_call" | custom-call | flops 10000000000 | bytes 20000000 | tf_op jit(solution)/shard_map/pallas_call | solution.py:110
  81.8 1.6 copy.32
  83.4 19.6 %all_to_all.39 = bf16[8,4,128,64]{2,0,3,1:T(8,128)(2,1)S(1)} all-to-all(bf16[8,4,128,64]{2,0,3,1:T(8,128)(2,1)S(1)} %copy.32), channel_id=1, replica_groups=mesh['seq'=8,'chan'=4] {'chan'}, dimensions={1} | all-to-all | bytes 1048576 | tf_op jit(solution)/shard_map/all_to_all | solution.py:158
  103.0 0.2 all_gather_reshape.3
  103.2 1.0 copy.33
  104.2 0.0 all-gather.5.cloned.1.call-update
  104.2 0.0 all-gather.7.cloned.1.call-done
  104.2 1.8 %copy.34 = bf16[4,8,64,512]{3,2,0,1:T(8,128)(2,1)S(1)} copy(bf16[4,8,64,512]{3,2,1,0:T(8,128)(2,1)} %bitcast.44) | data formatting | bytes 4194304 | tf_op jit(solution)/shard_map/reshape | solution.py:161
  106.0 33.2 %all-gather.5.cloned.1.call-done = bf16[8,1024,256]{2,1,0:T(8,128)(2,1)} async-done(((bf16[1,1024,256]{2,1,0:T(8,128)(2,1)}), bf16[8,1024,256]{2,1,0:T(8,128)(2,1)}) %all-gather.5.cloned.1.call-update) | async-done | bytes 4194320 | tf_op jit(solution)/shard_map/all_gather | solution.py:160
  139.2 4.5 %bitcast_convert_fusion = bf16[1024,512]{1,0:T(8,128)(2,1)S(1)} fusion(bf16[8,1024,256]{2,1,0:T(8,128)(2,1)} %all-gather.5.cloned.1.call-done, bf16[8,256,512]{2,1,0:T(8,128)(2,1)S(1)} %bitcast.45), kind=kOutput, calls=%fused_computation.3 | convolution fusion | flops 2148007936 | bytes 7340032 | tf_op jit(solution)/shard_map/stk,skn->tn/dot_general | solution.py:163
  143.7 17.9 %all_to_all.40 = bf16[8,128,512]{2,1,0:T(8,128)(2,1)S(1)} all-to-all(bf16[8,128,512]{2,1,0:T(8,128)(2,1)S(1)} %bitcast.49), channel_id=1, replica_groups=mesh['seq'=8,'chan'=4] {'seq'}, dimensions={0} | all-to-all | bytes 2097152 | tf_op jit(solution)/shard_map/all_to_all | solution.py:165
  161.6 1.1 copy.37
  (2 shorter events, 0.0 us)
Async XLA Ops:
  6.5 9.4 %copy-start = (f32[3,3,512]{2,1,0:T(4,128)S(1)}, f32[3,3,512]{2,1,0:T(4,128)}, u32[]{:S(2)}) copy-start(f32[3,3,512]{2,1,0:T(4,128)} %param.14) | copy-start | bytes 55300
  6.5 97.7 %all-gather.7.cloned.1.call-start = ((), (), s32[]{:S(2)}) async-start(), calls=%async_computation.4 | async-start | bytes 2621440 | tf_op jit(solution)/shard_map/all_gather | solution.py:139
  10.7 25.8 %all-to-all-start = ((bf16[512,8,64]{0,2,1:T(8,128)(2,1)}), bf16[512,8,64]{0,2,1:T(8,128)(2,1)S(1)}, u32[]{:S(2)}, u32[]{:S(2)}) async-start(bf16[512,8,64]{0,2,1:T(8,128)(2,1)} %bitcast.6), calls=%async_computation | async-start | bytes 1048576 | tf_op jit(solution)/shard_map/all_to_all | solution.py:141
  15.9 123.3 %all-gather.5.cloned.1.call-start = ((), (), s32[]{:S(2)}) async-start(), calls=%async_computation.3 | async-start | bytes 4718592 | tf_op jit(solution)/shard_map/all_gather | solution.py:160
  17.9 7.3 %copy-start.1 = (s32[512]{0:T(512)S(1)}, s32[512]{0:T(512)}, u32[]{:S(2)}) copy-start(s32[512]{0:T(512)} %param.11) | copy-start | bytes 6148
Sparse Core Ops, SparseCore 0:
  8.9 48.6 all-gather.6
  104.3 34.8 all-gather.4
where the time goes:
time: 170 us
  blocking collectives  46.8 us (28%)
  Pallas kernels  43.4 us (26%)
  waiting for transfers between devices  33.3 us (20%)
  local copies, waits for them, and re-layouts  16.6 us (10%)
  between operations  13.5 us (8%)
  matrix products  10.8 us (6%)
  starting transfers between devices  5.21 us (3%)
    pallas_call x1, Pallas kernels, run_operator(): pl.pallas_call(functools.partial(operator_kernel, width), out_shape=jax.S...  43.4 us
    all_gather x1, waiting for transfers between devices, body(): carried_all = lax.all_gather(blocks, 'seq', axis=0, tiled=False)  33.2 us
    all_to_all x1, blocking collectives, body(): lax.all_to_all(blocks, 'chan', split_axis=1, concat_axis=1, tiled=True)  19.6 us
    all_to_all x1, blocking collectives, body(): lax.all_to_all(mixed, 'seq', split_axis=0, concat_axis=2, tiled=True)  17.9 us
    all_gather x1, blocking collectives, body(): ids = lax.all_gather(token_ids, 'seq', axis=0, tiled=True)  9.33 us
    dot_general x1, matrix products, body(): jnp.einsum('vd,dgc->vgc', embed_table, mine(in_weight), preferred_element...  6.33 us
    all_to_all x1, starting transfers between devices, body(): lax.all_to_all(long_filter.astype(jnp.bfloat16), 'seq', split_axis=1, con...  5.17 us
    dot_general x1, matrix products, body(): jnp.einsum('stk,skn->tn', carried_all, weight, preferred_element_type=jnp...  4.5 us
  transfers between devices with their start and end apart: 3, of which 1 were waited for; matrix products, arithmetic and copies ran while one was open for 12% of the time, Pallas kernels for 26%

commit v1 on v0

--- a/solution.py
+++ b/solution.py
@@ -8,7 +8,6 @@
 from jax.experimental.pallas import tpu as pltpu
 from jax.sharding import PartitionSpec as P
 
-HIGHEST = lax.Precision.HIGHEST
 LANES = 128
 INNER = 64
 
@@ -27,16 +26,22 @@
         [np.concatenate([cosine, -sine], 2), np.concatenate([sine, cosine], 2)], 1
     )
     last = first.T / length
-    return (
-        first.astype(np.float32),
-        second.astype(np.float32),
-        np.swapaxes(second, 1, 2).astype(np.float32),
-        last.astype(np.float32),
-    )
+    return tuple(two_parts(m) for m in (first, second, np.swapaxes(second, 1, 2), last))
+
+
+def two_parts(matrix):
+    high = matrix.astype(jnp.bfloat16)
+    low = (matrix - high.astype(np.float64)).astype(jnp.bfloat16)
+    return np.concatenate([high, low], -1)
 
 
 def dot32(left, right):
-    return jnp.dot(left, right, precision=HIGHEST, preferred_element_type=jnp.float32)
+    high = right.astype(jnp.bfloat16)
+    low = (right - high.astype(jnp.float32)).astype(jnp.bfloat16)
+    depth = right.shape[0]
+    return jnp.dot(left, jnp.concatenate([high, high], 0), preferred_element_type=jnp.float32) + jnp.dot(
+        left[:, :depth], low, preferred_element_type=jnp.float32
+    )
 
 
 def operator_kernel(
@@ -70,13 +75,13 @@
         gate[rows, :] = branches[1]
         signal[rows, :] = branches[0] * branches[2] + filter_ref[rows, :].astype(jnp.float32)
 
-    @pl.loop(0, INNER, unroll=4)
+    @pl.loop(0, INNER, unroll=8)
     def _(n2):
         work[pl.ds(n2 * (2 * outer), 2 * outer), :] = dot32(
             first_ref[...], signal[pl.ds(n2, outer, stride=INNER), :]
         )
 
-    @pl.loop(0, outer, unroll=4)
+    @pl.loop(0, outer, unroll=8)
     def _(k1):
         real_rows = pl.ds(k1, INNER, stride=2 * outer)
         imag_rows = pl.ds(k1 + outer, INNER, stride=2 * outer)
@@ -93,7 +98,7 @@
         work[real_rows, :] = result[:INNER]
         work[imag_rows, :] = result[INNER:]
 
-    @pl.loop(0, INNER, unroll=4)
+    @pl.loop(0, INNER, unroll=8)
     def _(n2):
         rows = pl.ds(n2, outer, stride=INNER)
         convolved = dot32(last_ref[...], work[pl.ds(n2 * (2 * outer), 2 * outer), :])
@@ -138,9 +143,15 @@
     out_part = lax.dynamic_slice_in_dim(out_weight, place * columns, columns, 1)
     out_all = lax.all_gather(out_part, "chan", axis=0, tiled=False)
 
-    filters = lax.all_to_all(long_filter.astype(jnp.bfloat16), "seq", split_axis=1, concat_axis=0, tiled=True)
-    ids = lax.all_gather(token_ids, "seq", axis=0, tiled=True)
-    length = ids.shape[0]
+    digits = jnp.stack([token_ids // 256, token_ids % 256], -1).astype(jnp.bfloat16)
+    digits = jnp.broadcast_to(digits[:, None], (digits.shape[0], seq_count, 2))
+    sent = long_filter.astype(jnp.bfloat16).reshape(-1, seq_count, width)
+    sent = jnp.concatenate([sent, digits], -1)
+    received = lax.all_to_all(sent, "seq", split_axis=1, concat_axis=0, tiled=True)[:, 0]
+    length = received.shape[0]
+    filters = received[:, :width]
+    digits = received[:, width:].astype(jnp.int32)
+    ids = digits[:, 0] * 256 + digits[:, 1]
 
     def mine(array):
         return lax.dynamic_slice_in_dim(array, place * width, width, array.ndim - 1)

time: 170 us -> 151 us (0.89)
  Pallas kernels: 43.4 us -> 32.2 us
  blocking collectives: 46.8 us -> 36.6 us
  other arithmetic: 0 us -> 4.01 us
  local copies, waits for them, and re-layouts: 16.6 us -> 12.9 us
  waiting for transfers between devices: 33.3 us -> 35.4 us
    pallas_call x1, Pallas kernels: 43.4 us -> 32.2 us  [run_operator(): pl.pallas_call(functools.partial(operator_kernel, width), out_shape=jax.S...]
    all_gather x1 -> x0, blocking collectives: 9.33 us -> none  [body(): ids = lax.all_gather(token_ids, 'seq', axis=0, tiled=True)]
    unnamed x6, local copies, waits for them, and re-layouts: 3.32 us -> 1.3 us
    broadcast_in_dim x1, local copies, waits for them, and re-layouts: 1.99 us -> 0.01 us  [body(): digits = jnp.broadcast_to(digits[:, None], (digits.shape[0], seq_count, 2))]
    add x0 -> x1, other arithmetic: none -> 1.94 us  [body(): ids = digits[:, 0] * 256 + digits[:, 1]]
  transfers between devices with their start and end apart: 3 -> 3, of which waited for: 1 -> 2; matrix products, arithmetic and copies ran while one was open for 12% -> 13% of each run, Pallas kernels for 26% -> 21%
where the time goes in v1:
time: 151 us
  blocking collectives  36.6 us (24%)
  waiting for transfers between devices  35.4 us (23%)
  Pallas kernels  32.2 us (21%)
  between operations  13.5 us (9%)
  local copies, waits for them, and re-layouts  12.9 us (9%)
  matrix products  10.9 us (7%)
  starting transfers between devices  5.21 us (3%)
  other arithmetic  4.01 us (3%)
    all_gather x1, waiting for transfers between devices, body(): carried_all = lax.all_gather(blocks, 'seq', axis=0, tiled=False)  34.3 us
    pallas_call x1, Pallas kernels, run_operator(): pl.pallas_call(functools.partial(operator_kernel, width), out_shape=jax.S...  32.2 us
    all_to_all x1, blocking collectives, body(): lax.all_to_all(blocks, 'chan', split_axis=1, concat_axis=1, tiled=True)  18.7 us
    all_to_all x1, blocking collectives, body(): lax.all_to_all(mixed, 'seq', split_axis=0, concat_axis=2, tiled=True)  17.9 us
    dot_general x1, matrix products, body(): jnp.einsum('vd,dgc->vgc', embed_table, mine(in_weight), preferred_element...  6.35 us
    all_to_all x1, starting transfers between devices, body(): lax.all_to_all(sent, 'seq', split_axis=1, concat_axis=0, tiled=True)[:, 0]  5.17 us
    dot_general x1, matrix products, body(): jnp.einsum('stk,skn->tn', carried_all, weight, preferred_element_type=jnp...  4.5 us
  transfers between devices with their start and end apart: 3, of which 2 were waited for; matrix products, arithmetic and copies ran while one was open for 13% of the time, Pallas kernels for 21%

profile of v1, /device:TPU:0, one launch (start us, length us, event | category | flops | bytes accessed | tf_op | source)
XLA Modules:
  0.0 150.7 jit_solution(16593953665249944745)
XLA Ops:
  6.5 0.0 copy-start
  6.5 0.0 copy-start.1
  6.5 0.0 all-gather.6.cloned.1.call-start
  6.5 2.0 %constant_dynamic-slice_fusion = bf16[512,512]{1,0:T(8,128)(2,1)} fusion(bf16[512,4096]{1,0:T(8,128)(2,1)} %param.17, s32[]{:T(128)S(6)} %select_n.23), kind=kLoop, calls=%fused_computation.21 | loop fusion | bytes 1048580 | tf_op jit(solution)/shard_map/dynamic_slice | solution.py:143
  8.5 0.0 all-gather.6.cloned.1.call-update
  8.5 0.7 fusion.13
  9.3 0.0 copy-done.1
  9.3 0.2 copy.26
  9.5 0.9 pad_maximum_fusion
  10.4 5.2 %all-to-all-start = ((bf16[512,8,66]{0,2,1:T(8,128)(2,1)}), bf16[512,8,66]{0,2,1:T(8,128)(2,1)S(1)}, u32[]{:S(2)}, u32[]{:S(2)}) async-start(bf16[512,8,66]{0,2,1:T(8,128)(2,1)} %pad_maximum_fusion), calls=%async_computation | async-start | bytes 1179648 | tf_op jit(solution)/shard_map/all_to_all | solution.py:150
  15.6 0.0 all-gather.4.cloned.1.call-start
  15.6 0.8 dynamic-slice_bitcast_fusion
  16.4 0.6 pad.18.skip_ref
  17.0 0.0 copy-done
  17.0 0.1 constant_dynamic-slice_fusion.1
  17.0 0.6 reshape.44.taps_ref
  17.7 6.4 %fusion.8 = bf16[512,3,64]{0,2,1:T(8,128)(2,1)S(1)} fusion(bf16[512,4096]{1,0:T(8,128)(2,1)} %param.12, bf16[4096,3,512]{2,0,1:T(8,128)(2,1)} %param.13, s32[]{:T(128)S(6)} %select_n.22), kind=kOutput, calls=%fused_computation.7 | convolution fusion | flops 805404672 | bytes 7536644 | tf_op jit(solution)/shard_map/vd,dgc->vgc/dot_general | solution.py:159
  24.0 0.9 copy.29.table_ref
  25.0 1.0 all-to-all-done
  26.0 0.7 copy.27
  26.7 0.5 slice_convert_fusion
  27.2 1.4 pad.19.filter_ref
  28.5 1.9 %slice_add_fusion.ids_ref = s32[4096,1]{1,0:T(8,128)} fusion(s32[4096,2]{1,0:T(8,128)S(1)} %slice_convert_fusion), kind=kLoop, calls=%fused_computation.3 | loop fusion | flops 8192 | bytes 49152 | tf_op jit(solution)/shard_map/add | solution.py:154
  30.5 32.2 %shard_map.109 = bf16[4096,128]{1,0:T(8,128)(2,1)} custom-call(s32[4096,1]{1,0:T(8,128)} %slice_add_fusion.ids_ref, bf16[512,384]{1,0:T(8,128)(2,1)} %copy.29.table_ref, f32[9,128]{1,0:T(8,128)} %reshape.44.taps_ref, f32[1,128]{1,0:T(1,128)} %pad.18.skip_ref, bf16[4096,128]{1,0:T(8,128)(2,1)} %pad.19.filter_ref, bf16[128,128]{1,0:T(8,128)(2,1)} %constant.54.clone.first_ref, ...), custom_call_target="tpu_custom_call" | custom-call | flops 10000000000 | bytes 20000000 | tf_op jit(solution)/shard_map/pallas_call | solution.py:115
  62.7 1.6 %copy.30 = bf16[8,4,128,64]{2,0,3,1:T(8,128)(2,1)S(1)} copy(bf16[8,4,128,64]{3,2,1,0:T(8,128)(2,1)} %bitcast.51) | data formatting | bytes 1048576 | tf_op jit(solution)/shard_map/reshape | solution.py:168
  64.3 18.7 %all_to_all.35 = bf16[8,4,128,64]{2,0,3,1:T(8,128)(2,1)S(1)} all-to-all(bf16[8,4,128,64]{2,0,3,1:T(8,128)(2,1)S(1)} %copy.30), channel_id=1, replica_groups=mesh['seq'=8,'chan'=4] {'chan'}, dimensions={1} | all-to-all | bytes 1048576 | tf_op jit(solution)/shard_map/all_to_all | solution.py:169
  83.0 0.2 all_gather_reshape.3
  83.2 1.0 copy.31
  84.2 0.0 all-gather.4.cloned.1.call-update
  84.3 0.0 all-gather.6.cloned.1.call-done
  84.3 1.8 %copy.32 = bf16[4,8,64,512]{3,2,0,1:T(8,128)(2,1)S(1)} copy(bf16[4,8,64,512]{3,2,1,0:T(8,128)(2,1)} %bitcast.47) | data formatting | bytes 4194304 | tf_op jit(solution)/shard_map/reshape | solution.py:172
  86.0 34.3 %all-gather.4.cloned.1.call-done = bf16[8,1024,256]{2,1,0:T(8,128)(2,1)} async-done(((bf16[1,1024,256]{2,1,0:T(8,128)(2,1)}), bf16[8,1024,256]{2,1,0:T(8,128)(2,1)}) %all-gather.4.cloned.1.call-update) | async-done | bytes 4194320 | tf_op jit(solution)/shard_map/all_gather | solution.py:171
  120.3 4.5 %bitcast_convert_fusion = bf16[1024,512]{1,0:T(8,128)(2,1)S(1)} fusion(bf16[8,1024,256]{2,1,0:T(8,128)(2,1)} %all-gather.4.cloned.1.call-done, bf16[8,256,512]{2,1,0:T(8,128)(2,1)S(1)} %bitcast.48), kind=kOutput, calls=%fused_computation.5 | convolution fusion | flops 2148007936 | bytes 7340032 | tf_op jit(solution)/shard_map/stk,skn->tn/dot_general | solution.py:174
  124.8 17.9 %all_to_all.36 = bf16[8,128,512]{2,1,0:T(8,128)(2,1)S(1)} all-to-all(bf16[8,128,512]{2,1,0:T(8,128)(2,1)S(1)} %bitcast.52), channel_id=1, replica_groups=mesh['seq'=8,'chan'=4] {'seq'}, dimensions={0} | all-to-all | bytes 2097152 | tf_op jit(solution)/shard_map/all_to_all | solution.py:176
  142.7 1.1 copy.35
  (6 shorter events, 0.1 us)
Async XLA Ops:
  6.5 10.4 %copy-start = (f32[3,3,512]{2,1,0:T(4,128)S(1)}, f32[3,3,512]{2,1,0:T(4,128)}, u32[]{:S(2)}) copy-start(f32[3,3,512]{2,1,0:T(4,128)} %param.14) | copy-start | bytes 55300
  6.5 2.7 %copy-start.1 = (f32[512,512]{1,0:T(8,128)S(1)}, f32[512,512]{1,0:T(8,128)}, u32[]{:S(2)}) copy-start(f32[512,512]{1,0:T(8,128)} %param.15) | copy-start | bytes 3145732
  6.5 77.7 %all-gather.6.cloned.1.call-start = ((), (), s32[]{:S(2)}) async-start(), calls=%async_computation.4 | async-start | bytes 2621440 | tf_op jit(solution)/shard_map/all_gather | solution.py:144
  10.4 15.6 %all-to-all-start = ((bf16[512,8,66]{0,2,1:T(8,128)(2,1)}), bf16[512,8,66]{0,2,1:T(8,128)(2,1)S(1)}, u32[]{:S(2)}, u32[]{:S(2)}) async-start(bf16[512,8,66]{0,2,1:T(8,128)(2,1)} %pad_maximum_fusion), calls=%async_computation | async-start | bytes 1179648 | tf_op jit(solution)/shard_map/all_to_all | solution.py:150
  15.6 104.8 %all-gather.4.cloned.1.call-start = ((), (), s32[]{:S(2)}) async-start(), calls=%async_computation.3 | async-start | bytes 4718592 | tf_op jit(solution)/shard_map/all_gather | solution.py:171
Sparse Core Ops, SparseCore 0:
  8.9 48.6 all-gather.5
  84.4 35.8 all-gather.3

commit v2 on v1

--- a/solution.py
+++ b/solution.py
@@ -138,10 +138,14 @@
     seq_count, chan_count = lax.axis_size("seq"), lax.axis_size("chan")
     depth = embed_table.shape[1]
     width = in_weight.shape[2] // seq_count
-    columns = out_weight.shape[1] // seq_count
-
-    out_part = lax.dynamic_slice_in_dim(out_weight, place * columns, columns, 1)
-    out_all = lax.all_gather(out_part, "chan", axis=0, tiled=False)
+    chips = seq_count // 2
+    columns = out_weight.shape[1] // chips
+    cores = [[2 * chip, 2 * chip + 1] for chip in range(chips)]
+    planes = [[2 * chip + core for chip in range(chips)] for core in range(2)]
+
+    out_part = lax.dynamic_slice_in_dim(out_weight, place * (columns // 2), columns // 2, 1)
+    out_part = lax.all_gather(out_part, "chan", axis=0, tiled=False)
+    out_all = lax.all_gather(out_part, "seq", axis=0, tiled=False, axis_index_groups=cores)
 
     digits = jnp.stack([token_ids // 256, token_ids % 256], -1).astype(jnp.bfloat16)
     digits = jnp.broadcast_to(digits[:, None], (digits.shape[0], seq_count, 2))
@@ -165,15 +169,20 @@
     carried = run_operator(ids[:, None], table, taps, skip, to_lanes(filters, width), width)[:, :width]
 
     rows = length // (seq_count * chan_count)
-    blocks = carried.reshape(seq_count, chan_count, rows, width)
-    blocks = lax.all_to_all(blocks, "chan", split_axis=1, concat_axis=1, tiled=True)
-    blocks = blocks.transpose(0, 2, 1, 3).reshape(seq_count * rows, chan_count * width)
-    carried_all = lax.all_gather(blocks, "seq", axis=0, tiled=False)
-    weight = out_all.reshape(chan_count, seq_count, width, columns).transpose(1, 0, 2, 3)
-    weight = weight.reshape(seq_count, chan_count * width, columns)
-    mixed = jnp.einsum("stk,skn->tn", carried_all, weight, preferred_element_type=jnp.float32)
-    mixed = mixed.astype(jnp.bfloat16).reshape(seq_count, rows, columns)
-    mixed = lax.all_to_all(mixed, "seq", split_axis=0, concat_axis=2, tiled=True)
+    blocks = carried.reshape(chips, 2, chan_count, rows, width)
+    blocks = lax.all_to_all(blocks, "chan", split_axis=2, concat_axis=2, tiled=True)
+    blocks = blocks.transpose(1, 0, 3, 2, 4).reshape(2, chips * rows, chan_count * width)
+    blocks = lax.all_to_all(
+        blocks, "seq", split_axis=0, concat_axis=0, tiled=True, axis_index_groups=cores
+    )
+    carried_all = lax.all_gather(blocks, "seq", axis=0, tiled=False, axis_index_groups=planes)
+    weight = out_all.reshape(2, chan_count, chips, 2, width, columns // 2).transpose(2, 3, 1, 4, 0, 5)
+    weight = weight.reshape(chips, 2, chan_count * width, columns)
+    mixed = jnp.einsum("pqtk,pqkn->tn", carried_all, weight, preferred_element_type=jnp.float32)
+    mixed = mixed.astype(jnp.bfloat16).reshape(chips, rows, columns)
+    mixed = lax.all_to_all(
+        mixed, "seq", split_axis=0, concat_axis=2, tiled=True, axis_index_groups=planes
+    )
     return mixed[0]
 
 

time: 151 us -> 193 us (1.28)
  waiting for transfers between devices: 35.4 us -> 57.9 us
  local copies, waits for them, and re-layouts: 12.9 us -> 29.6 us
  blocking collectives: 36.6 us -> 38.6 us
    all_gather x2 -> x3, waiting for transfers between devices: 34.3 us -> 57.9 us  [the longest x1 39.6 us: body(): out_part = lax.all_gather(out_part, 'chan', axis=0, tiled=False)]
    transpose x0 -> x2, local copies, waits for them, and re-layouts: none -> 8.69 us  [the longest x1 8.51 us: body(): out_all.reshape(2, chan_count, chips, 2, width, columns // 2)]
    reshape x2 -> x3, local copies, waits for them, and re-layouts: 3.36 us -> 9.46 us  [the longest x1 7.71 us: body(): weight = weight.reshape(chips, 2, chan_count * width, columns)]
    all_to_all x2 -> x3, blocking collectives: 36.6 us -> 38.6 us  [the longest x1 17.6 us: body(): lax.all_to_all(blocks, 'chan', split_axis=2, concat_axis=2, tiled=True)]
  transfers between devices with their start and end apart: 3 -> 4, of which waited for: 2 -> 2; matrix products, arithmetic and copies ran while one was open for 13% -> 18% of each run, Pallas kernels for 21% -> 17%
where the time goes in v2:
time: 193 us; the launch traced here: 192 us
  waiting for transfers between devices  57.9 us (30%)
  blocking collectives  38.6 us (20%)
  Pallas kernels  32.2 us (17%)
  local copies, waits for them, and re-layouts  29.6 us (15%)
  between operations  13.2 us (7%)
  matrix products  11.1 us (6%)
  starting transfers between devices  5.25 us (3%)
  other arithmetic  4.01 us (2%)
    all_gather x1, waiting for transfers between devices, body(): out_part = lax.all_gather(out_part, 'chan', axis=0, tiled=False)  39.6 us
    pallas_call x1, Pallas kernels, run_operator(): pl.pallas_call(functools.partial(operator_kernel, width), out_shape=jax.S...  32.2 us
    all_gather x1, waiting for transfers between devices, body(): lax.all_gather(blocks, 'seq', axis=0, tiled=False, axis_index_groups=planes)  18.3 us
    all_to_all x1, blocking collectives, body(): lax.all_to_all(blocks, 'chan', split_axis=2, concat_axis=2, tiled=True)  17.6 us
    all_to_all x1, blocking collectives, body(): lax.all_to_all(mixed, 'seq', split_axis=0, concat_axis=2, tiled=True, axi...  16.8 us
    transpose x1, local copies, waits for them, and re-layouts, body(): out_all.reshape(2, chan_count, chips, 2, width, columns // 2)  8.51 us
    reshape x1, local copies, waits for them, and re-layouts, body(): weight = weight.reshape(chips, 2, chan_count * width, columns)  7.71 us
    dot_general x1, matrix products, body(): jnp.einsum('vd,dgc->vgc', embed_table, mine(in_weight), preferred_element...  5.93 us
  transfers between devices with their start and end apart: 4, of which 2 were waited for; matrix products, arithmetic and copies ran while one was open for 18% of the time, Pallas kernels for 17%

profile of v2, /device:TPU:0, one launch (start us, length us, event | category | flops | bytes accessed | tf_op | source)
XLA Modules:
  0.0 191.9 jit_solution(13903376616898650272)
XLA Ops:
  6.5 0.0 copy-start
  6.5 0.0 all-gather.9.cloned.1.call-start
  6.5 1.9 constant_dynamic-slice_fusion
  8.4 0.0 all-gather.9.cloned.1.call-update
  8.5 0.7 fusion.13
  9.2 1.4 copy.24
  10.6 0.9 pad_maximum_fusion
  11.5 5.2 %all-to-all-start = ((bf16[512,8,66]{0,2,1:T(8,128)(2,1)}), bf16[512,8,66]{0,2,1:T(8,128)(2,1)S(1)}, u32[]{:S(2)}, u32[]{:S(2)}) async-start(bf16[512,8,66]{0,2,1:T(8,128)(2,1)} %pad_maximum_fusion), calls=%async_computation | async-start | bytes 1179648 | tf_op jit(solution)/shard_map/all_to_all | solution.py:154
  16.7 0.0 all-gather.11.cloned.1.call-start
  16.7 0.8 dynamic-slice_bitcast_fusion
  17.5 0.5 pad.18.skip_ref
  18.0 39.6 %all-gather.9.cloned.1.call-done = bf16[2048,512]{1,0:T(8,128)(2,1)} async-done(((bf16[512,512]{1,0:T(8,128)(2,1)}), bf16[2048,512]{1,0:T(8,128)(2,1)}) %all-gather.9.cloned.1.call-update) | async-done | bytes 2097168 | tf_op jit(solution)/shard_map/all_gather | solution.py:147
  57.6 0.0 all-gather.11.cloned.1.call-update
  57.6 0.0 all-gather.7.cloned.1.call-start
  57.7 0.0 copy-done
  57.7 0.1 constant_dynamic-slice_fusion.1
  57.8 0.6 reshape.47.taps_ref
  58.4 5.9 %fusion.8 = bf16[512,3,64]{0,2,1:T(8,128)(2,1)S(1)} fusion(bf16[512,4096]{1,0:T(8,128)(2,1)} %param.12, bf16[4096,3,512]{2,0,1:T(8,128)(2,1)} %param.13, s32[]{:T(128)S(6)} %select_n.22), kind=kOutput, calls=%fused_computation.7 | convolution fusion | flops 805404672 | bytes 7536644 | tf_op jit(solution)/shard_map/vd,dgc->vgc/dot_general | solution.py:163
  64.4 0.9 copy.27.table_ref
  65.3 0.0 all-to-all-done
  65.3 0.7 copy.25
  66.0 1.4 pad.19.filter_ref
  67.3 0.5 slice_convert_fusion
  67.8 1.9 %slice_add_fusion.ids_ref = s32[4096,1]{1,0:T(8,128)} fusion(s32[4096,2]{1,0:T(8,128)S(1)} %slice_convert_fusion), kind=kLoop, calls=%fused_computation.3 | loop fusion | flops 8192 | bytes 49152 | tf_op jit(solution)/shard_map/add | solution.py:158
  69.7 32.2 %shard_map.109 = bf16[4096,128]{1,0:T(8,128)(2,1)} custom-call(s32[4096,1]{1,0:T(8,128)} %slice_add_fusion.ids_ref, bf16[512,384]{1,0:T(8,128)(2,1)} %copy.27.table_ref, f32[9,128]{1,0:T(8,128)} %reshape.47.taps_ref, f32[1,128]{1,0:T(1,128)} %pad.18.skip_ref, bf16[4096,128]{1,0:T(8,128)(2,1)} %pad.19.filter_ref, bf16[128,128]{1,0:T(8,128)(2,1)} %constant.54.clone.first_ref, ...), custom_call_target="tpu_custom_call" | custom-call | flops 10000000000 | bytes 20000000 | tf_op jit(solution)/shard_map/pallas_call | solution.py:115
  102.0 1.6 copy.28
  103.5 17.6 %all_to_all.40 = bf16[4,2,4,128,64]{3,0,4,1,2:T(4,128)(2,1)S(1)} all-to-all(bf16[4,2,4,128,64]{3,0,4,1,2:T(4,128)(2,1)S(1)} %copy.28), channel_id=1, replica_groups=mesh['seq'=8,'chan'=4] {'chan'}, dimensions={2} | all-to-all | bytes 1048576 | tf_op jit(solution)/shard_map/all_to_all | solution.py:173
  121.1 0.2 copy.29
  121.3 0.2 reshape.49
  121.5 4.2 %all_to_all.41 = bf16[2,512,256]{1,2,0:T(8,128)(2,1)S(1)} all-to-all(bf16[2,512,256]{1,2,0:T(8,128)(2,1)S(1)} %reshape.49), channel_id=1, replica_groups={{0,4},{8,12},{16,20},{24,28},{1,5},{9,13},{17,21},{25,29},{2,6},{10,14}..., dimensions={0} | all-to-all | bytes 1048576 | tf_op jit(solution)/shard_map/all_to_all | solution.py:175
  125.7 1.0 copy.30
  126.7 0.0 all-gather.7.cloned.1.call-update
  126.7 0.0 all-gather.11.cloned.1.call-done
  126.7 8.5 %copy.31 = bf16[4,2,4,64,2,512]{5,4,3,2,1,0:T(2,128)(2,1)} copy(bf16[4,2,4,64,2,512]{5,3,1,0,2,4:T(8,128)(2,1)} %bitcast.43) | data formatting | bytes 8388608 | tf_op jit(solution)/shard_map/transpose | solution.py:179
  135.2 7.7 %reshape.51 = bf16[4,2,256,1024]{3,2,1,0:T(8,128)(2,1)} reshape(bf16[4,2,4,64,2,512]{5,4,3,2,1,0:T(2,128)(2,1)} %copy.31) | data formatting | bytes 8388608 | tf_op jit(solution)/shard_map/reshape | solution.py:180
  143.0 18.3 %all-gather.7.cloned.1.call-done = bf16[8,512,256]{2,1,0:T(8,128)(2,1)} async-done(((bf16[2,512,256]{2,1,0:T(8,128)(2,1)}), bf16[8,512,256]{2,1,0:T(8,128)(2,1)}) %all-gather.7.cloned.1.call-update) | async-done | bytes 2097168 | tf_op jit(solution)/shard_map/all_gather | solution.py:178
  161.2 5.1 %bitcast_convert_fusion = bf16[512,1024]{1,0:T(8,128)(2,1)S(1)} fusion(bf16[4,2,512,256]{3,2,1,0:T(8,128)(2,1)} %bitcast.53, bf16[4,2,256,1024]{3,2,1,0:T(8,128)(2,1)} %reshape.51), kind=kOutput, calls=%fused_computation.5 | convolution fusion | flops 2148007936 | bytes 7340032 | tf_op jit(solution)/shard_map/pqtk,pqkn->tn/dot_general | solution.py:181
  166.4 16.8 %all_to_all.42 = bf16[4,128,1024]{2,1,0:T(8,128)(2,1)S(1)} all-to-all(bf16[4,128,1024]{2,1,0:T(8,128)(2,1)S(1)} %bitcast.52), channel_id=1, replica_groups={{0,8,16,24},{4,12,20,28},{1,9,17,25},{5,13,21,29},{2,10,18,26},{6,14,22..., dimensions={0} | all-to-all | bytes 2097152 | tf_op jit(solution)/shard_map/all_to_all | solution.py:183
  183.2 0.8 copy.32
  184.0 1.3 copy.35
  (6 shorter events, 0.1 us)
Async XLA Ops:
  6.5 51.1 %copy-start = (f32[3,3,512]{2,1,0:T(4,128)S(1)}, f32[3,3,512]{2,1,0:T(4,128)}, u32[]{:S(2)}) copy-start(f32[3,3,512]{2,1,0:T(4,128)} %param.14) | copy-start | bytes 55300
  6.5 51.1 %all-gather.9.cloned.1.call-start = ((), (), s32[]{:S(2)}) async-start(), calls=%async_computation.5 | async-start | bytes 2621440 | tf_op jit(solution)/shard_map/all_gather | solution.py:147
  11.5 53.8 %all-to-all-start = ((bf16[512,8,66]{0,2,1:T(8,128)(2,1)}), bf16[512,8,66]{0,2,1:T(8,128)(2,1)S(1)}, u32[]{:S(2)}, u32[]{:S(2)}) async-start(bf16[512,8,66]{0,2,1:T(8,128)(2,1)} %pad_maximum_fusion), calls=%async_computation | async-start | bytes 1179648 | tf_op jit(solution)/shard_map/all_to_all | solution.py:154
  16.7 110.0 %all-gather.11.cloned.1.call-start = ((), (), s32[]{:S(2)}) async-start(), calls=%async_computation.6 | async-start | bytes 6291456 | tf_op jit(solution)/shard_map/all_gather | solution.py:148
  57.6 103.6 %all-gather.7.cloned.1.call-start = ((), (), s32[]{:S(2)}) async-start(), calls=%async_computation.4 | async-start | bytes 2621440 | tf_op jit(solution)/shard_map/all_gather | solution.py:178
Sparse Core Ops, SparseCore 0:
  8.9 48.6 all-gather.8
  59.1 12.3 all-gather.10
  126.8 34.3 all-gather.6

commit v3 on v1

--- a/solution.py
+++ b/solution.py
@@ -166,15 +166,19 @@
 
     rows = length // (seq_count * chan_count)
     blocks = carried.reshape(seq_count, chan_count, rows, width)
-    blocks = lax.all_to_all(blocks, "chan", split_axis=1, concat_axis=1, tiled=True)
-    blocks = blocks.transpose(0, 2, 1, 3).reshape(seq_count * rows, chan_count * width)
-    carried_all = lax.all_gather(blocks, "seq", axis=0, tiled=False)
     weight = out_all.reshape(chan_count, seq_count, width, columns).transpose(1, 0, 2, 3)
     weight = weight.reshape(seq_count, chan_count * width, columns)
-    mixed = jnp.einsum("stk,skn->tn", carried_all, weight, preferred_element_type=jnp.float32)
-    mixed = mixed.astype(jnp.bfloat16).reshape(seq_count, rows, columns)
-    mixed = lax.all_to_all(mixed, "seq", split_axis=0, concat_axis=2, tiled=True)
-    return mixed[0]
+    half = rows // 2
+    results = []
+    for part in range(2):
+        block = blocks[:, :, part * half : (part + 1) * half]
+        block = lax.all_to_all(block, "chan", split_axis=1, concat_axis=1, tiled=True)
+        block = block.transpose(0, 2, 1, 3).reshape(seq_count * half, chan_count * width)
+        carried_all = lax.all_gather(block, "seq", axis=0, tiled=False)
+        mixed = jnp.einsum("stk,skn->tn", carried_all, weight, preferred_element_type=jnp.float32)
+        mixed = mixed.astype(jnp.bfloat16).reshape(seq_count, half, columns)
+        results.append(lax.all_to_all(mixed, "seq", split_axis=0, concat_axis=2, tiled=True)[0])
+    return jnp.concatenate(results, 0)
 
 
 def solution(mesh):

time: 151 us -> 166 us (1.099)
  waiting for transfers between devices: 35.4 us -> 48.2 us
  blocking collectives: 36.6 us -> 25.2 us
  starting transfers between devices: 5.21 us -> 12.3 us
  local copies, waits for them, and re-layouts: 12.9 us -> 16.1 us
  matrix products: 10.9 us -> 13.2 us
    all_to_all x2, blocking collectives: 36.6 us -> 25.2 us  [body(): lax.all_to_all(block, 'chan', split_axis=1, concat_axis=1, tiled=True)]
    all_to_all x0 -> x2, waiting for transfers between devices: none -> 9.63 us  [body(): lax.all_to_all(mixed, 'seq', split_axis=0, concat_axis=2, tiled=True)[0]]
    all_to_all x0 -> x2, starting transfers between devices: none -> 6.99 us  [body(): lax.all_to_all(mixed, 'seq', split_axis=0, concat_axis=2, tiled=True)[0]]
    all_gather x1 -> x2, waiting for transfers between devices: 34.3 us -> 38.5 us  [body(): carried_all = lax.all_gather(block, 'seq', axis=0, tiled=False)]
    dot_general x1 -> x2, matrix products: 4.5 us -> 7.26 us  [body(): jnp.einsum('stk,skn->tn', carried_all, weight, preferred_element_type=jnp...]
    unnamed x6 -> x11, local copies, waits for them, and re-layouts: 1.3 us -> 3.09 us
    another operation x2 -> x4, local copies, waits for them, and re-layouts: 1.22 us -> 2.95 us  [body(): carried_all = lax.all_gather(block, 'seq', axis=0, tiled=False)]
  transfers between devices with their start and end apart: 3 -> 6, of which waited for: 2 -> 3; matrix products, arithmetic and copies ran while one was open for 13% -> 18% of each run, Pallas kernels for 21% -> 19%
where the time goes in v3:
time: 166 us; the launch traced here: 165 us
  waiting for transfers between devices  48.2 us (29%)
  Pallas kernels  32.2 us (19%)
  blocking collectives  25.2 us (15%)
  local copies, waits for them, and re-layouts  16.1 us (10%)
  between operations  13.3 us (8%)
  matrix products  13.2 us (8%)
  starting transfers between devices  12.3 us (7%)
  other arithmetic  5.07 us (3%)
    all_gather x2, waiting for transfers between devices, body(): carried_all = lax.all_gather(block, 'seq', axis=0, tiled=False)  38.5 us
    pallas_call x1, Pallas kernels, run_operator(): pl.pallas_call(functools.partial(operator_kernel, width), out_shape=jax.S...  32.2 us
    all_to_all x2, blocking collectives, body(): lax.all_to_all(block, 'chan', split_axis=1, concat_axis=1, tiled=True)  25.2 us
    all_to_all x2, waiting for transfers between devices, body(): lax.all_to_all(mixed, 'seq', split_axis=0, concat_axis=2, tiled=True)[0]  9.63 us
    dot_general x2, matrix products, body(): jnp.einsum('stk,skn->tn', carried_all, weight, preferred_element_type=jnp...  7.26 us
    all_to_all x2, starting transfers between devices, body(): lax.all_to_all(mixed, 'seq', split_axis=0, concat_axis=2, tiled=True)[0]  6.99 us
    dot_general x1, matrix products, body(): jnp.einsum('vd,dgc->vgc', embed_table, mine(in_weight), preferred_element...  5.94 us
    all_to_all x1, starting transfers between devices, body(): lax.all_to_all(sent, 'seq', split_axis=1, concat_axis=0, tiled=True)[:, 0]  5.17 us
  transfers between devices with their start and end apart: 6, of which 3 were waited for; matrix products, arithmetic and copies ran while one was open for 18% of the time, Pallas kernels for 19%

profile of v3, /device:TPU:0, one launch (start us, length us, event | category | flops | bytes accessed | tf_op | source)
XLA Modules:
  0.0 165.5 jit_solution(2573567639234754986)
XLA Ops:
  6.5 0.0 copy-start
  6.5 0.7 fusion.15
  7.3 1.4 copy.38
  8.7 0.9 pad_maximum_fusion.1
  9.6 5.2 %all-to-all-start = ((bf16[512,8,66]{0,2,1:T(8,128)(2,1)}), bf16[512,8,66]{0,2,1:T(8,128)(2,1)S(1)}, u32[]{:S(2)}, u32[]{:S(2)}) async-start(bf16[512,8,66]{0,2,1:T(8,128)(2,1)} %pad_maximum_fusion.1), calls=%async_computation | async-start | bytes 1179648 | tf_op jit(solution)/shard_map/all_to_all | solution.py:150
  14.8 0.0 all-gather.9.cloned.1.call-start
  14.8 1.9 %constant_dynamic-slice_fusion = bf16[512,512]{1,0:T(8,128)(2,1)} fusion(bf16[512,4096]{1,0:T(8,128)(2,1)} %param.17, s32[]{:T(128)S(6)} %select_n.23), kind=kLoop, calls=%fused_computation.25 | loop fusion | bytes 1048580 | tf_op jit(solution)/shard_map/dynamic_slice | solution.py:143
  16.7 0.0 all-gather.9.cloned.1.call-update
  16.7 0.0 all-gather.5.cloned.1.call-start
  16.8 5.9 %fusion.10 = bf16[512,3,64]{0,2,1:T(8,128)(2,1)S(1)} fusion(bf16[512,4096]{1,0:T(8,128)(2,1)} %param.12, bf16[4096,3,512]{2,0,1:T(8,128)(2,1)} %param.13, s32[]{:T(128)S(6)} %select_n.22), kind=kOutput, calls=%fused_computation.10 | convolution fusion | flops 805404672 | bytes 7536644 | tf_op jit(solution)/shard_map/vd,dgc->vgc/dot_general | solution.py:159
  22.8 1.0 copy.41.table_ref
  23.7 0.0 copy-done
  23.7 0.1 constant_dynamic-slice_fusion.1
  23.8 0.6 reshape.48.taps_ref
  24.4 0.8 dynamic-slice_bitcast_fusion
  25.2 0.5 pad.18.skip_ref
  25.7 0.0 all-to-all-done
  25.7 0.7 copy.39
  26.4 0.5 slice_convert_fusion
  26.9 1.4 pad.19.filter_ref
  28.2 1.9 %slice_add_fusion.ids_ref = s32[4096,1]{1,0:T(8,128)} fusion(s32[4096,2]{1,0:T(8,128)S(1)} %slice_convert_fusion), kind=kLoop, calls=%fused_computation.3 | loop fusion | flops 8192 | bytes 49152 | tf_op jit(solution)/shard_map/add | solution.py:154
  30.2 32.2 %shard_map.109 = bf16[4096,128]{1,0:T(8,128)(2,1)} custom-call(s32[4096,1]{1,0:T(8,128)} %slice_add_fusion.ids_ref, bf16[512,384]{1,0:T(8,128)(2,1)} %copy.41.table_ref, f32[9,128]{1,0:T(8,128)} %reshape.48.taps_ref, f32[1,128]{1,0:T(1,128)} %pad.18.skip_ref, bf16[4096,128]{1,0:T(8,128)(2,1)} %pad.19.filter_ref, bf16[128,128]{1,0:T(8,128)(2,1)} %constant.54.clone.first_ref, ...), custom_call_target="tpu_custom_call" | custom-call | flops 10000000000 | bytes 20000000 | tf_op jit(solution)/shard_map/pallas_call | solution.py:115
  62.3 1.3 fusion.19
  63.7 0.4 reshape.63
  64.1 14.2 %all_to_all.55 = bf16[4,2,16384]{2,1,0:T(2,128)(2,1)S(1)} all-to-all(bf16[4,2,16384]{2,1,0:T(2,128)(2,1)S(1)} %reshape.63), channel_id=1, replica_groups=mesh['seq'=8,'chan'=4] {'chan'}, dimensions={0} | all-to-all | bytes 524288 | tf_op jit(solution)/shard_map/all_to_all | solution.py:175
  78.3 0.3 reshape.64
  78.7 0.4 copy.51
  79.1 1.1 reshape.59
  80.2 0.0 all-gather.5.cloned.1.call-update
  80.2 0.0 all-gather.7.cloned.1.call-start
  80.3 0.4 reshape.61
  80.7 11.0 %all_to_all.56 = bf16[4,2,16384]{2,1,0:T(2,128)(2,1)S(1)} all-to-all(bf16[4,2,16384]{2,1,0:T(2,128)(2,1)S(1)} %reshape.61), channel_id=1, replica_groups=mesh['seq'=8,'chan'=4] {'chan'}, dimensions={0} | all-to-all | bytes 524288 | tf_op jit(solution)/shard_map/all_to_all | solution.py:175
  91.7 0.3 reshape.62
  92.1 0.4 copy.52
  92.6 1.1 reshape.60
  93.6 0.0 all-gather.7.cloned.1.call-update
  93.6 0.0 all-gather.9.cloned.1.call-done
  93.7 1.8 %copy.45 = bf16[4,8,64,512]{3,2,0,1:T(8,128)(2,1)S(1)} copy(bf16[4,8,64,512]{3,2,1,0:T(8,128)(2,1)} %bitcast.72) | data formatting | bytes 4194304 | tf_op jit(solution)/shard_map/reshape | solution.py:169
  95.4 12.0 %all-gather.5.cloned.1.call-done = bf16[8,512,256]{2,1,0:T(8,128)(2,1)} async-done(((bf16[1,512,256]{2,1,0:T(8,128)(2,1)}), bf16[8,512,256]{2,1,0:T(8,128)(2,1)}) %all-gather.5.cloned.1.call-update) | async-done | bytes 2097168 | tf_op jit(solution)/shard_map/all_gather | solution.py:177
  107.5 3.6 %fusion.3 = bf16[512,512]{1,0:T(8,128)(2,1)} fusion(bf16[8,512,256]{2,1,0:T(8,128)(2,1)} %all-gather.5.cloned.1.call-done, bf16[8,256,512]{2,1,0:T(8,128)(2,1)S(1)} %bitcast.73), kind=kOutput, calls=%fused_computation.7 | convolution fusion | flops 1074003968 | bytes 4718592 | tf_op jit(solution)/shard_map/stk,skn->tn/dot_general | solution.py:178
  111.1 3.5 %all-to-all-start.2 = ((bf16[8,64,512]{2,1,0:T(8,128)(2,1)}), bf16[8,64,512]{2,1,0:T(8,128)(2,1)S(1)}, u32[]{:S(2)}, u32[]{:S(2)}) async-start(bf16[8,64,512]{2,1,0:T(8,128)(2,1)} %bitcast.14), calls=%async_computation.2 | async-start | bytes 1048576 | tf_op jit(solution)/shard_map/all_to_all | solution.py:180
  114.6 26.4 %all-gather.7.cloned.1.call-done = bf16[8,512,256]{2,1,0:T(8,128)(2,1)} async-done(((bf16[1,512,256]{2,1,0:T(8,128)(2,1)}), bf16[8,512,256]{2,1,0:T(8,128)(2,1)}) %all-gather.7.cloned.1.call-update) | async-done | bytes 2097168 | tf_op jit(solution)/shard_map/all_gather | solution.py:177
  141.0 3.6 %fusion.4 = bf16[512,512]{1,0:T(8,128)(2,1)} fusion(bf16[8,512,256]{2,1,0:T(8,128)(2,1)} %all-gather.7.cloned.1.call-done, bf16[8,256,512]{2,1,0:T(8,128)(2,1)S(1)} %bitcast.74), kind=kOutput, calls=%fused_computation.8 | convolution fusion | flops 1074003968 | bytes 4718592 | tf_op jit(solution)/shard_map/stk,skn->tn/dot_general | solution.py:178
  144.7 0.0 all-to-all-done.2
  144.7 3.5 %all-to-all-start.4 = ((bf16[8,64,512]{2,1,0:T(8,128)(2,1)}), bf16[8,64,512]{2,1,0:T(8,128)(2,1)S(1)}, u32[]{:S(2)}, u32[]{:S(2)}) async-start(bf16[8,64,512]{2,1,0:T(8,128)(2,1)} %bitcast.20), calls=%async_computation.4 | async-start | bytes 1048576 | tf_op jit(solution)/shard_map/all_to_all | solution.py:180
  148.2 9.6 %all-to-all-done.4 = bf16[8,64,512]{2,1,0:T(8,128)(2,1)S(1)} async-done(((bf16[8,64,512]{2,1,0:T(8,128)(2,1)}), bf16[8,64,512]{2,1,0:T(8,128)(2,1)S(1)}, u32[]{:S(2)}, u32[]{:S(2)}) %all-to-all-start.4) | async-done | bytes 524320 | tf_op jit(solution)/shard_map/all_to_all | solution.py:180
  157.9 1.1 pad_maximum_fusion
  (12 shorter events, 0.3 us)
Async XLA Ops:
  6.5 17.2 %copy-start = (f32[3,3,512]{2,1,0:T(4,128)S(1)}, f32[3,3,512]{2,1,0:T(4,128)}, u32[]{:S(2)}) copy-start(f32[3,3,512]{2,1,0:T(4,128)} %param.14) | copy-start | bytes 55300
  9.6 16.1 %all-to-all-start = ((bf16[512,8,66]{0,2,1:T(8,128)(2,1)}), bf16[512,8,66]{0,2,1:T(8,128)(2,1)S(1)}, u32[]{:S(2)}, u32[]{:S(2)}) async-start(bf16[512,8,66]{0,2,1:T(8,128)(2,1)} %pad_maximum_fusion.1), calls=%async_computation | async-start | bytes 1179648 | tf_op jit(solution)/shard_map/all_to_all | solution.py:150
  14.8 78.9 %all-gather.9.cloned.1.call-start = ((), (), s32[]{:S(2)}) async-start(), calls=%async_computation.7 | async-start | bytes 2621440 | tf_op jit(solution)/shard_map/all_gather | solution.py:144
  16.7 90.7 %all-gather.5.cloned.1.call-start = ((), (), s32[]{:S(2)}) async-start(), calls=%async_computation.5 | async-start | bytes 2359296 | tf_op jit(solution)/shard_map/all_gather | solution.py:177
  80.2 60.8 %all-gather.7.cloned.1.call-start = ((), (), s32[]{:S(2)}) async-start(), calls=%async_computation.6 | async-start | bytes 2359296 | tf_op jit(solution)/shard_map/all_gather | solution.py:177
  111.1 33.6 %all-to-all-start.2 = ((bf16[8,64,512]{2,1,0:T(8,128)(2,1)}), bf16[8,64,512]{2,1,0:T(8,128)(2,1)S(1)}, u32[]{:S(2)}, u32[]{:S(2)}) async-start(bf16[8,64,512]{2,1,0:T(8,128)(2,1)} %bitcast.14), calls=%async_computation.2 | async-start | bytes 1048576 | tf_op jit(solution)/shard_map/all_to_all | solution.py:180
  144.7 13.2 %all-to-all-start.4 = ((bf16[8,64,512]{2,1,0:T(8,128)(2,1)}), bf16[8,64,512]{2,1,0:T(8,128)(2,1)S(1)}, u32[]{:S(2)}, u32[]{:S(2)}) async-start(bf16[8,64,512]{2,1,0:T(8,128)(2,1)} %bitcast.20), calls=%async_computation.4 | async-start | bytes 1048576 | tf_op jit(solution)/shard_map/all_to_all | solution.py:180
Sparse Core Ops, SparseCore 0:
  17.2 47.6 all-gather.8
  80.3 27.0 all-gather.4
  109.4 31.6 all-gather.6
